TPU v7x, 128 devices: a whole 4x4x4 slice. The times are simulated.
128 devices in a mesh: dp: 4 (over x_lo, core), tensor: 32 (over z, y, x_hi).
Axes of the slice: x: 4 (x_hi: 2, x_lo: 2; x = x_hi * 2 + x_lo), y: 4, z: 4, core: 2. Of those that a mesh axis runs over, the one named last changes fastest.
Arguments:
- tokens: bfloat16 [2048, 4096], P(('dp', 'tensor')), may hold values from -6 to 6
- cotangent: bfloat16 [2048, 4096], P(('dp', 'tensor')), may hold values from -6 to 6
- gate_weight: bfloat16 [4096, 14336], P(None, 'tensor'), may hold values from -0.09375 to 0.09375
- up_weight: bfloat16 [4096, 14336], P(None, 'tensor'), may hold values from -0.09375 to 0.09375
- down_weight: bfloat16 [14336, 4096], P('tensor'), may hold values from -0.046875 to 0.046875
Outputs:
- output: bfloat16 [2048, 4096], P(('dp', 'tensor'))
- input_grad: bfloat16 [2048, 4096], P(('dp', 'tensor'))
- gate_grad: bfloat16 [4096, 14336], P('dp', 'tensor')
- up_grad: bfloat16 [4096, 14336], P('dp', 'tensor')
- down_grad: bfloat16 [14336, 4096], P('tensor', 'dp')
All inputs are finite; a program needn't handle non-finite values.
Results may differ from a plain program's by a relative error of at most 0.005.
Values may be sent and summed in bfloat16 or wider, within the bound.
A program may use at most 128 MiB of HBM per device.

v0:
```python
import jax
import jax.numpy as jnp
from jax import lax
from jax.sharding import PartitionSpec as P


def contract_rows(left, right):
    return lax.dot_general(
        left, right, (((0,), (0,)), ((), ())), preferred_element_type=jnp.float32
    )


def contract_cols(left, right):
    return lax.dot_general(
        left, right, (((1,), (1,)), ((), ())), preferred_element_type=jnp.float32
    )


def body(tokens, cotangent, gate_weight, up_weight, down_weight):
    gathered = lax.all_gather(tokens, "tensor", axis=0, tiled=True)
    gate = jnp.dot(gathered, gate_weight, preferred_element_type=jnp.float32)
    up = jnp.dot(gathered, up_weight, preferred_element_type=jnp.float32)
    sig = jax.nn.sigmoid(gate)
    act = gate * sig
    hidden = (act * up).astype(jnp.bfloat16)
    output = lax.psum_scatter(
        jnp.dot(hidden, down_weight, preferred_element_type=jnp.float32),
        "tensor",
        scatter_dimension=0,
        tiled=True,
    ).astype(jnp.bfloat16)
    cot_group = lax.all_gather(cotangent, "tensor", axis=0, tiled=True)
    dhidden = contract_cols(cot_group, down_weight)
    dgate = (dhidden * up * sig * (1.0 + gate * (1.0 - sig))).astype(jnp.bfloat16)
    dup = (dhidden * act).astype(jnp.bfloat16)
    input_grad = lax.psum_scatter(
        contract_cols(dgate, gate_weight) + contract_cols(dup, up_weight),
        "tensor",
        scatter_dimension=0,
        tiled=True,
    ).astype(jnp.bfloat16)
    part_g = contract_rows(gathered, dgate)
    part_u = contract_rows(gathered, dup)
    part_d = contract_rows(hidden, cot_group)
    sum_g, sum_u, sum_d = (
        lax.psum_scatter(part_g, "dp", scatter_dimension=0, tiled=True),
        lax.psum_scatter(part_u, "dp", scatter_dimension=0, tiled=True),
        lax.psum_scatter(part_d, "dp", scatter_dimension=1, tiled=True),
    )
    return (
        output,
        input_grad,
        sum_g.astype(jnp.bfloat16),
        sum_u.astype(jnp.bfloat16),
        sum_d.astype(jnp.bfloat16),
    )


def solution(mesh):
    placed = (
        P(("dp", "tensor"), None),
        P(("dp", "tensor"), None),
        P(None, "tensor"),
        P(None, "tensor"),
        P("tensor", None),
    )
    return jax.shard_map(
        body,
        mesh=mesh,
        in_specs=placed,
        out_specs=(
            P(("dp", "tensor"), None),
            P(("dp", "tensor"), None),
            P("dp", "tensor"),
            P("dp", "tensor"),
            P("tensor", "dp"),
        ),
        check_vma=False,
    )
```

profile of v0, /device:TPU:0, one launch (start us, length us, event | category | flops | bytes accessed | tf_op | source)
XLA Modules:
  0.0 847.5 jit_solution(17069291051607220393)
XLA Ops:
  7.2 0.0 all-gather.3.cloned.1.call-start
  7.2 0.7 all-gather.3.cloned.1.call-update
  7.9 0.0 all-gather.5.cloned.1.call-start
  7.9 0.7 all-gather.5.cloned.1.call-update
  8.6 0.0 reduce-scatter.14.cloned.1.call-start
  8.7 85.4 %all-gather.3.cloned.1.call-done = bf16[512,4096]{1,0:T(8,128)(2,1)} async-done(((bf16[16,4096]{1,0:T(8,128)(2,1)}), bf16[512,4096]{1,0:T(8,128)(2,1)}) %all-gather.3.cloned.1.call-update) | async-done | bytes 4194320 | tf_op jit(solution)/shard_map/all_gather | solution.py:20
  94.1 0.0 copy-start
  94.1 0.0 copy-start.3
  94.1 5.5 fusion.2
  99.6 0.0 copy-done
  99.6 0.1 copy-done.3
  99.7 2.1 fusion.1
  101.8 74.7 %all-gather.5.cloned.1.call-done = bf16[512,4096]{1,0:T(8,128)(2,1)} async-done(((bf16[16,4096]{1,0:T(8,128)(2,1)}), bf16[512,4096]{1,0:T(8,128)(2,1)}) %all-gather.5.cloned.1.call-update) | async-done | bytes 4194320 | tf_op jit(solution)/shard_map/all_gather | solution.py:32
  176.5 0.0 copy-start.1
  176.5 5.8 multiply_convert_fusion
  182.3 0.0 copy-done.1
  182.4 5.2 fusion.5
  187.5 0.0 reduce-scatter.14.cloned.1.call-update
  187.5 0.0 reduce-scatter.12.cloned.1.call-start
  187.6 7.3 convolution_bitcast_fusion
  194.9 0.0 reduce-scatter.12.cloned.1.call-update
  194.9 0.0 reduce-scatter.10.cloned.1.call-start
  194.9 7.9 convolution_bitcast_fusion.1
  202.9 0.0 reduce-scatter.10.cloned.1.call-update
  202.9 0.2 reduce-scatter.8.cloned.1.call-start
  203.1 0.0 copy-start.2
  203.1 4.6 fusion.4
  207.7 0.0 copy-done.2
  207.8 5.9 convolution_add_fusion
  213.7 0.0 reduce-scatter.8.cloned.1.call-update
  213.7 0.0 reduce-scatter.6.cloned.1.call-start
  213.7 7.6 fusion.3
  221.4 0.0 reduce-scatter.6.cloned.1.call-update
  221.4 36.1 %reduce-scatter.14.cloned.1.call-done = f32[448,1024]{1,0:T(8,128)} async-done(((f32[448,4096]{1,0:T(8,128)}), f32[448,1024]{1,0:T(8,128)}) %reduce-scatter.14.cloned.1.call-update) | async-done | bytes 1835024 | tf_op jit(solution)/shard_map/reduce_scatter | solution.py:48
  257.5 2.6 convert_element_type.31
  260.1 71.8 %reduce-scatter.12.cloned.1.call-done = f32[1024,448]{0,1:T(8,128)} async-done(((f32[4096,448]{0,1:T(8,128)}), f32[1024,448]{0,1:T(8,128)}) %reduce-scatter.12.cloned.1.call-update) | async-done | bytes 1835024 | tf_op jit(solution)/shard_map/reduce_scatter | solution.py:47
  331.8 2.6 convert_element_type.30
  334.4 71.7 %reduce-scatter.10.cloned.1.call-done = f32[1024,448]{0,1:T(8,128)} async-done(((f32[4096,448]{0,1:T(8,128)}), f32[1024,448]{0,1:T(8,128)}) %reduce-scatter.10.cloned.1.call-update) | async-done | bytes 1835024 | tf_op jit(solution)/shard_map/reduce_scatter | solution.py:46
  406.1 2.6 convert_element_type.29
  408.7 215.7 %reduce-scatter.8.cloned.1.call-done = f32[16,4096]{1,0:T(8,128)} async-done(((f32[512,4096]{1,0:T(8,128)}), f32[16,4096]{1,0:T(8,128)}) %reduce-scatter.8.cloned.1.call-update) | async-done | bytes 262160 | tf_op jit(solution)/shard_map/reduce_scatter | solution.py:36
  624.4 1.6 convert_element_type.28
  626.0 213.1 %reduce-scatter.6.cloned.1.call-done = f32[16,4096]{1,0:T(8,128)} async-done(((f32[512,4096]{1,0:T(8,128)}), f32[16,4096]{1,0:T(8,128)}) %reduce-scatter.6.cloned.1.call-update) | async-done | bytes 262160 | tf_op jit(solution)/shard_map/reduce_scatter | solution.py:26
  839.1 1.6 convert_element_type.25
Async XLA Ops:
  7.2 86.9 %all-gather.3.cloned.1.call-start = ((), (), s32[]{:S(2)}) async-start(), calls=%async_computation.5 | async-start | bytes 4325376 | tf_op jit(solution)/shard_map/all_gather | solution.py:20
  7.9 168.6 %all-gather.5.cloned.1.call-start = ((), (), s32[]{:S(2)}) async-start(), calls=%async_computation.7 | async-start | bytes 4325376 | tf_op jit(solution)/shard_map/all_gather | solution.py:32
  8.6 248.9 %reduce-scatter.14.cloned.1.call-start = ((), (), s32[]{:S(2)}) async-start(), calls=%async_computation.11 | async-start | bytes 9175040 | tf_op jit(solution)/shard_map/reduce_scatter | solution.py:48
  94.1 5.5 copy-start
  94.1 5.6 copy-start.3
  176.5 5.9 copy-start.1
  187.5 144.3 %reduce-scatter.12.cloned.1.call-start = ((), (), s32[]{:S(2)}) async-start(), calls=%async_computation.10 | async-start | bytes 9175040 | tf_op jit(solution)/shard_map/reduce_scatter | solution.py:47
  194.9 211.2 %reduce-scatter.10.cloned.1.call-start = ((), (), s32[]{:S(2)}) async-start(), calls=%async_computation.9 | async-start | bytes 9175040 | tf_op jit(solution)/shard_map/reduce_scatter | solution.py:46
  202.9 421.5 %reduce-scatter.8.cloned.1.call-start = ((), (), s32[]{:S(2)}) async-start(), calls=%async_computation.8 | async-start | bytes 8650752 | tf_op jit(solution)/shard_map/reduce_scatter | solution.py:36
  203.1 4.6 copy-start.2
  213.7 625.4 %reduce-scatter.6.cloned.1.call-start = ((), (), s32[]{:S(2)}) async-start(), calls=%async_computation.6 | async-start | bytes 8650752 | tf_op jit(solution)/shard_map/reduce_scatter | solution.py:26
Sparse Core Ops, SparseCore 0:
  11.1 82.9 all-gather.2
  97.1 79.3 all-gather.4
  187.7 69.8 reduce-scatter.13
  259.8 72.0 reduce-scatter.11
  334.1 71.9 reduce-scatter.9
  408.4 215.9 reduce-scatter.7
  626.8 212.2 reduce-scatter.5
where the time goes:
time: 848 us
  waiting for transfers between devices  770 us (91%)
  matrix products  52 us (6%)
  between operations  14.2 us (2%)
  other arithmetic  10.9 us (1%)
    reduce_scatter x1, waiting for transfers between devices, body(): lax.psum_scatter(contract_cols(dgate, gate_weight) + contract_cols(dup, u...  216 us
    reduce_scatter x1, waiting for transfers between devices, body(): lax.psum_scatter(jnp.dot(hidden, down_weight, preferred_element_type=jnp....  213 us
    all_gather x1, waiting for transfers between devices, body(): gathered = lax.all_gather(tokens, 'tensor', axis=0, tiled=True)  85.4 us
    all_gather x1, waiting for transfers between devices, body(): cot_group = lax.all_gather(cotangent, 'tensor', axis=0, tiled=True)  74.7 us
    reduce_scatter x1, waiting for transfers between devices, body(): lax.psum_scatter(part_u, 'dp', scatter_dimension=0, tiled=True)  71.8 us
    reduce_scatter x1, waiting for transfers between devices, body(): lax.psum_scatter(part_g, 'dp', scatter_dimension=0, tiled=True)  71.7 us
    reduce_scatter x1, waiting for transfers between devices, body(): lax.psum_scatter(part_d, 'dp', scatter_dimension=1, tiled=True)  36.1 us
    dot_general x3, matrix products, contract_rows(): lax.dot_general(left, right, (((0,), (0,)), ((), ())), preferred_element_...  20.4 us
  transfers between devices with their start and end apart: 7, of which 7 were waited for; matrix products, arithmetic and copies ran while one was open for 6% of the time, Pallas kernels for 0%

commit v1 on v0

v1 whole, which is shorter than its diff:
```python
import jax
import jax.numpy as jnp
from jax import lax
from jax.experimental import pallas as pl
from jax.experimental.pallas import tpu as pltpu
from jax.sharding import PartitionSpec as P

MESH = pl.DeviceIdType.MESH
BF16, F32 = jnp.bfloat16, jnp.float32
T, D, H, Q = 512, 4096, 448, 1024


def mm(a, b):
    return jnp.dot(a, b, preferred_element_type=F32)


def mm_nt(a, b):
    return lax.dot_general(a, b, (((1,), (1,)), ((), ())), preferred_element_type=F32)


def kernel(
    tok, cot, wg, wu, wd,
    out, ig, gg, ug, dg,
    X, WG, WU, WD, gate, up, dhid, hid, dgate, dup, hidT, dgT, duT,
    PS, R1, RF, R2, R3, TS, TO, SO, OB, WB, CR, XR,
    ls, gs, gr, ss, sr, cs, cr, xs, xr,
):
    dp, t = lax.axis_index("dp"), lax.axis_index("tensor")
    xl, c = dp // 2, lax.rem(dp, 2)
    z, y, xh = t // 8, lax.rem(t // 2, 4), lax.rem(t, 2)

    def ring(v, off):
        return lax.rem(v + (off + 4) % 4, 4)

    def dev(zz, yy, hh=None):
        return (dp, zz * 8 + yy * 2 + (xh if hh is None else hh))

    x_pair = ((1 - xl) * 2 + c, t)
    core_pair = (xl * 2 + 1 - c, t)
    h_pair = dev(z, y, 1 - xh)
    my_row = pl.multiple_of(xh * 16, 16)
    pair_row = pl.multiple_of((1 - xh) * 16, 16)
    OFFS = (1, -1, 2)

    def at(h, a, b):
        return (b, a) if h == 0 else (a, b)

    me_a, me_b = (y, z), (z, y)

    def peer(h, da=0, db=0):
        return dev(*at(h, ring(me_a[h], da), ring(me_b[h], db)))

    started = []

    def send(src, dst, s, r, to):
        cp = pltpu.make_async_remote_copy(
            src_ref=src, dst_ref=dst, send_sem=s, recv_sem=r, device_id=to, device_id_type=MESH
        )
        cp.start()
        started.append(cp)
        return cp

    def arrived(ref, r):
        pltpu.make_async_copy(ref, ref, r).wait()

    loads = []
    for arr, ref in enumerate((tok, cot)):
        for q in range(4):
            cp = pltpu.make_async_copy(
                ref.at[:, pl.ds(q * Q, Q)], X.at[arr * 4 + q, z, y, pl.ds(my_row, 16)], ls.at[arr * 4 + q]
            )
            cp.start()
            loads.append(cp)
    wloads = [pltpu.make_async_copy(wg, WG, ls.at[8]), pltpu.make_async_copy(wu, WU, ls.at[9])]
    for q in range(4):
        wloads.append(pltpu.make_async_copy(wd.at[:, pl.ds(q * Q, Q)], WD.at[q], ls.at[10 + q]))
    for cp in wloads:
        cp.start()

    barrier = pltpu.get_barrier_semaphore()
    peers = [x_pair, core_pair, h_pair]
    for off in OFFS:
        peers += [dev(ring(z, off), y), dev(z, ring(y, off))]
    for p in peers:
        pl.semaphore_signal(barrier, inc=1, device_id=p, device_id_type=MESH)
    pl.semaphore_wait(barrier, len(peers))

    base = (0, 2, 4 + (1 - xl) * 2, 4 + xl * 2)

    def blk(u, h, a, b):
        return X.at[(base[u] + h,) + at(h, a, b)]

    def sub(u, h, a, b, row):
        return X.at[(base[u] + h,) + at(h, a, b) + (pl.ds(row, 16),)]

    def gsend(u, i, ref, to):
        send(ref, ref, gs.at[u, i], gr.at[u, i], to)

    def g_start(u):
        ref = X.at[pl.ds(base[u], 2), z, y, pl.ds(my_row, 16)]
        gsend(u, 0, ref, h_pair)
        for s, off in enumerate(OFFS):
            for h in range(2):
                gsend(u, 1 + h * 6 + s, sub(u, h, me_a[h], me_b[h], my_row), peer(h, da=off))

    def g_spread(u, s):
        for h in range(2):
            a = me_a[h] if s == 0 else ring(me_a[h], -OFFS[s - 1])
            for d, off in enumerate((1, -1)):
                gsend(u, 13 + h * 8 + s * 2 + d, blk(u, h, a, me_b[h]), peer(h, db=off))

    def g_own(u):
        arrived(X.at[pl.ds(base[u], 2), z, y, pl.ds(pair_row, 16)], gr.at[u, 0])
        for s, off in enumerate(OFFS):
            for h in range(2):
                gsend(u, 4 + h * 6 + s, sub(u, h, me_a[h], me_b[h], pair_row), peer(h, da=off))
        g_spread(u, 0)

    def g_mid(u, s):
        off = OFFS[s - 1]
        for h in range(2):
            a = ring(me_a[h], -off)
            arrived(sub(u, h, a, me_b[h], my_row), gr.at[u, 1 + h * 6 + s - 1])
            arrived(sub(u, h, a, me_b[h], pair_row), gr.at[u, 4 + h * 6 + s - 1])
        g_spread(u, s)

    def g_forward(u, s):
        for h in range(2):
            a = me_a[h] if s == 0 else ring(me_a[h], -OFFS[s - 1])
            for d, off in enumerate((1, -1)):
                b = ring(me_b[h], -off)
                i = h * 8 + s * 2 + d
                arrived(blk(u, h, a, b), gr.at[u, 13 + i])
                gsend(u, 29 + i, sub(u, h, a, b, d * 16), peer(h, db=off))

    def g_done(u):
        for s in range(4):
            for h in range(2):
                a = me_a[h] if s == 0 else ring(me_a[h], -OFFS[s - 1])
                for d in range(2):
                    arrived(sub(u, h, a, ring(me_b[h], 2), d * 16), gr.at[u, 29 + h * 8 + s * 2 + d])

    def rows_of(i, r):
        return X[i, pl.ds(2 * r, 2)].reshape(256, Q)

    def gate_up(w):
        for q in (2 * w, 2 * w + 1):
            def step(r, _):
                x = rows_of(q, r)
                rows = pl.ds(pl.multiple_of(r * 256, 256), 256)
                g = mm(x, WG[pl.ds(q * Q, Q), :])
                u = mm(x, WU[pl.ds(q * Q, Q), :])
                if q == 0:
                    gate[rows, :] = g
                    up[rows, :] = u
                else:
                    gate[rows, :] += g
                    up[rows, :] += u
                return 0

            lax.fori_loop(0, 2, step, 0)

    def hidden():
        def step(r, _):
            rows = pl.ds(pl.multiple_of(r * 32, 32), 32)
            g = gate[rows, :]
            hid[rows, :] = (g * jax.nn.sigmoid(g) * up[rows, :]).astype(BF16)
            return 0

        lax.fori_loop(0, 16, step, 0)

    def backward():
        def step(r, _):
            rows = pl.ds(pl.multiple_of(r * 32, 32), 32)
            g, dh = gate[rows, :], dhid[rows, :]
            sig = jax.nn.sigmoid(g)
            dgate[rows, :] = (dh * up[rows, :] * sig * (1.0 + g * (1.0 - sig))).astype(BF16)
            dup[rows, :] = (dh * (g * sig)).astype(BF16)
            return 0

        lax.fori_loop(0, 16, step, 0)

    def transpose(src, dst):
        for r in range(4):
            dst[:, r * 128:(r + 1) * 128] = src[r * 128:(r + 1) * 128, :].astype(F32).T.astype(BF16)

    def output_part(q):
        def step(r, _):
            rows = pl.ds(pl.multiple_of(r * 256, 256), 256)
            PS[q, pl.ds(2 * r, 2)] = mm(hid[rows, :], WD[q]).astype(BF16).reshape(2, 4, 32, Q)
            return 0

        lax.fori_loop(0, 2, step, 0)

    def dhidden_part(u, first):
        for h in range(2):
            def step(r, _):
                rows = pl.ds(pl.multiple_of(r * 256, 256), 256)
                v = mm_nt(rows_of(base[u] + h, r), WD[base[u] - 4 + h])
                if first and h == 0:
                    dhid[rows, :] = v
                else:
                    dhid[rows, :] += v
                return 0

            lax.fori_loop(0, 2, step, 0)

    def input_part(q):
        def step(r, _):
            rows = pl.ds(pl.multiple_of(r * 256, 256), 256)
            v = mm_nt(dgate[rows, :], WG[pl.ds(q * Q, Q), :]) + mm_nt(dup[rows, :], WU[pl.ds(q * Q, Q), :])
            PS[4 + q, pl.ds(2 * r, 2)] = v.astype(BF16).reshape(2, 4, 32, Q)
            return 0

        lax.fori_loop(0, 2, step, 0)

    def chunk(v, h, b, row, n):
        tail = (pl.ds(row, n), slice(None))
        i = (v // 2) * 4 + (v % 2) * 2 + h
        return (i, b, slice(None)) + tail if h == 0 else (i, slice(None), b) + tail

    def s_first(v):
        for h in range(2):
            for d, off in enumerate((1, -1)):
                k = h * 6 + d * 3
                far, near = ring(me_b[h], 2), ring(me_b[h], off)
                send(PS.at[chunk(v, h, far, d * 16, 16)], RF.at[v, h, d], ss.at[v, k], sr.at[v, k], peer(h, db=off))
                o = (1 - d) * 16
                send(
                    PS.at[chunk(v, h, near, o, 16)], R1.at[v, h, d, :, pl.ds(o, 16)],
                    ss.at[v, k + 1], sr.at[v, k + 1], peer(h, db=off),
                )

    def s_join(v):
        for h in range(2):
            for d, off in enumerate((1, -1)):
                k = h * 6 + d * 3
                near, o = ring(me_b[h], off), d * 16
                arrived(RF.at[v, h, d], sr.at[v, k])
                RF[v, h, d] = (
                    RF[v, h, d].astype(F32) + PS[chunk(v, h, near, o, 16)].astype(F32)
                ).astype(BF16)
                send(
                    RF.at[v, h, d], R1.at[v, h, d, :, pl.ds(o, 16)],
                    ss.at[v, k + 2], sr.at[v, k + 2], peer(h, db=off),
                )

    def s_second(v):
        for h in range(2):
            for d in range(2):
                k = h * 6 + d * 3
                arrived(R1.at[v, h, d, :, pl.ds((1 - d) * 16, 16)], sr.at[v, k + 1])
                arrived(R1.at[v, h, d, :, pl.ds(d * 16, 16)], sr.at[v, k + 2])
            i = (v // 2) * 4 + (v % 2) * 2 + h

            def total(a):
                own = PS[(i,) + at(h, a, me_b[h])].astype(F32)
                return own + R1[v, h, 0, a].astype(F32) + R1[v, h, 1, a].astype(F32)

            for s, off in enumerate(OFFS):
                a = ring(me_a[h], off)
                mine = (i,) + at(h, a, me_b[h])
                PS[mine] = total(a).astype(BF16)
                k = 12 + h * 3 + s
                send(PS.at[mine], R2.at[v, h, s], ss.at[v, k], sr.at[v, k], peer(h, da=off))
            SO[v, h] = total(me_a[h])

    def s_third(v):
        for h in range(2):
            for s in range(3):
                arrived(R2.at[v, h, s], sr.at[v, 12 + h * 3 + s])
            SO[v, h] = (
                SO[v, h] + R2[v, h, 0].astype(F32) + R2[v, h, 1].astype(F32) + R2[v, h, 2].astype(F32)
            )
            TO[v, h] = SO[v, h, pl.ds(my_row, 16)]
            TS[v, h] = SO[v, h, pl.ds(pair_row, 16)].astype(BF16)
        send(TS.at[v], R3.at[v], ss.at[v, 18], sr.at[v, 18], h_pair)

    stores = []

    def s_finish(v):
        arrived(R3.at[v], sr.at[v, 18])
        for h in range(2):
            q = (v % 2) * 2 + h
            OB[v // 2, :, q * Q:(q + 1) * Q] = (TO[v, h] + R3[v, h].astype(F32)).astype(BF16)
        if v % 2 == 1:
            cp = pltpu.make_async_copy(OB.at[v // 2], (out, ig)[v // 2], ls.at[14 + v // 2])
            cp.start()
            stores.append(cp)

    lhs, x0 = (hidT, dgT, duT), (4, 0, 0)
    jobs = {}

    def w_part(j):
        arr, w = j % 3, (1 - xl) if j < 3 else xl
        if j >= 2:
            jobs[j - 2].wait_send()
            started[:] = [cp for cp in started if cp is not jobs[j - 2]]

        def step(k, _):
            quarter = w * 2 + jnp.where(k == 0, 1 - c, c)
            slot = jnp.where(k == 0, 6 + j % 2, j)
            for n in range(2):
                xb = X[x0[arr] + quarter, :, :, :, n * 512:(n + 1) * 512].reshape(T, 512)
                WB[slot, :, n * 512:(n + 1) * 512] = mm(lhs[arr][...], xb).astype(BF16)
            return 0

        lax.fori_loop(0, 2, step, 0)
        jobs[j] = send(WB.at[6 + j % 2], CR.at[j], cs.at[j], cr.at[j], core_pair)

    def w_cross(j):
        arrived(CR.at[j], cr.at[j])

        def step(r, _):
            rows = pl.ds(pl.multiple_of(r * 64, 64), 64)
            WB[j, rows, :] = (WB[j, rows, :].astype(F32) + CR[j, rows, :].astype(F32)).astype(BF16)
            return 0

        lax.fori_loop(0, 7, step, 0)
        send(WB.at[j], XR.at[j], xs.at[j], xr.at[j], x_pair)

    def w_finish(arr):
        j = 3 + arr
        arrived(CR.at[j], cr.at[j])
        arrived(XR.at[arr], xr.at[arr])
        if arr == 0:
            def step(r, _):
                rows = pl.ds(pl.multiple_of(r * 64, 64), 64)
                v = WB[j, rows, :].astype(F32) + CR[j, rows, :].astype(F32) + XR[arr, rows, :].astype(F32)
                WB[j, rows, :] = v.astype(BF16)
                return 0

            lax.fori_loop(0, 7, step, 0)
            cp = pltpu.make_async_copy(WB.at[j], dg, ls.at[16])
        else:
            buf = (WG, WU)[arr - 1]
            for n in range(8):
                cols = slice(n * 128, (n + 1) * 128)
                v = WB[j, :, cols].astype(F32) + CR[j, :, cols].astype(F32) + XR[arr, :, cols].astype(F32)
                buf[cols, :] = v.T.astype(BF16)
            cp = pltpu.make_async_copy(buf.at[pl.ds(0, Q)], (gg, ug)[arr - 1], ls.at[16 + arr])
        cp.start()
        stores.append(cp)

    for cp in loads:
        cp.wait()
    g_start(0)
    g_own(0)
    g_start(1)
    for s in (1, 2, 3):
        g_mid(0, s)
    g_forward(0, 0)
    g_own(1)
    for s in (1, 2, 3):
        g_forward(0, s)
    g_start(2)
    for s in (1, 2, 3):
        g_mid(1, s)
    g_done(0)
    for cp in wloads:
        cp.wait()
    gate_up(0)
    g_own(2)
    for s in range(4):
        g_forward(1, s)
    g_start(3)
    for s in (1, 2, 3):
        g_mid(2, s)
    g_done(1)
    gate_up(1)
    g_own(3)
    for s in range(4):
        g_forward(2, s)
    hidden()
    for s in (1, 2, 3):
        g_mid(3, s)
    transpose(hid, hidT)
    g_done(2)
    w_part(0)
    for s in range(4):
        g_forward(3, s)
    w_cross(0)
    output_part(0)
    output_part(1)
    s_first(0)
    output_part(2)
    output_part(3)
    s_first(1)
    dhidden_part(2, True)
    g_done(3)
    dhidden_part(3, False)
    backward()
    transpose(dgate, dgT)
    w_part(1)
    transpose(dup, duT)
    s_join(0)
    w_part(2)
    w_cross(1)
    s_join(1)
    input_part(0)
    input_part(1)
    w_cross(2)
    s_first(2)
    s_second(0)
    input_part(2)
    input_part(3)
    s_first(3)
    s_second(1)
    w_part(3)
    s_join(2)
    s_third(0)
    w_part(4)
    s_join(3)
    s_third(1)
    w_part(5)
    s_finish(0)
    s_finish(1)
    s_second(2)
    w_finish(0)
    s_second(3)
    s_third(2)
    s_third(3)
    s_finish(2)
    s_finish(3)
    w_finish(1)
    w_finish(2)
    for cp in started:
        cp.wait_send()
    for cp in stores:
        cp.wait()


def body(tokens, cotangent, gate_weight, up_weight, down_weight):
    any_spec = pl.BlockSpec(memory_space=pl.ANY)
    vm, dma = pltpu.VMEM, pltpu.SemaphoreType.DMA
    blocks = (4, 4, 32, Q)
    return pl.pallas_call(
        kernel,
        out_shape=(
            jax.ShapeDtypeStruct((16, D), BF16),
            jax.ShapeDtypeStruct((16, D), BF16),
            jax.ShapeDtypeStruct((Q, H), BF16),
            jax.ShapeDtypeStruct((Q, H), BF16),
            jax.ShapeDtypeStruct((H, Q), BF16),
        ),
        in_specs=[any_spec] * 5,
        out_specs=[any_spec] * 5,
        scratch_shapes=[
            vm((8,) + blocks, BF16),
            vm((D, H), BF16), vm((D, H), BF16), vm((4, H, Q), BF16),
            vm((T, H), F32), vm((T, H), F32), vm((T, H), F32),
            vm((T, H), BF16), vm((T, H), BF16), vm((T, H), BF16),
            vm((H, T), BF16), vm((H, T), BF16), vm((H, T), BF16),
            vm((8,) + blocks, BF16),
            vm((4, 2, 2, 4, 32, Q), BF16),
            vm((4, 2, 2, 4, 16, Q), BF16),
            vm((4, 2, 3, 32, Q), BF16),
            vm((4, 2, 16, Q), BF16), vm((4, 2, 16, Q), BF16),
            vm((4, 2, 16, Q), F32), vm((4, 2, 32, Q), F32),
            vm((2, 16, D), BF16),
            vm((8, H, Q), BF16), vm((6, H, Q), BF16), vm((3, H, Q), BF16),
            dma((19,)), dma((4, 45)), dma((4, 45)), dma((4, 19)), dma((4, 19)),
            dma((6,)), dma((6,)), dma((3,)), dma((3,)),
        ],
        compiler_params=pltpu.CompilerParams(
            collective_id=0, has_side_effects=True, vmem_limit_bytes=62 * 1024 * 1024
        ),
        cost_estimate=pl.CostEstimate(flops=17_000_000_000, bytes_accessed=15_000_000, transcendentals=460_000),
    )(tokens, cotangent, gate_weight, up_weight, down_weight)


def solution(mesh):
    placed = (
        P(("dp", "tensor"), None),
        P(("dp", "tensor"), None),
        P(None, "tensor"),
        P(None, "tensor"),
        P("tensor", None),
    )
    return jax.shard_map(
        body,
        mesh=mesh,
        in_specs=placed,
        out_specs=(
            P(("dp", "tensor"), None),
            P(("dp", "tensor"), None),
            P("dp", "tensor"),
            P("dp", "tensor"),
            P("tensor", "dp"),
        ),
        check_vma=False,
    )
```

time: 848 us -> 159 us (0.19)
  waiting for transfers between devices: 770 us -> 0 us
  Pallas kernels: 0 us -> 139 us
  matrix products: 52 us -> 0 us
  local copies, waits for them, and re-layouts: 0.08 us -> 19.7 us
  between operations: 14.2 us -> 0.67 us
  other arithmetic: 10.9 us -> 0 us
    reduce_scatter x5 -> x0, waiting for transfers between devices: 608 us -> none  [the longest x1 216 us: body(): lax.psum_scatter(contract_cols(dgate, gate_weight) + contract_cols(dup, u...]
    all_gather x2 -> x0, waiting for transfers between devices: 160 us -> none  [the longest x1 85.4 us: body(): gathered = lax.all_gather(tokens, 'tensor', axis=0, tiled=True)]
    pallas_call x0 -> x1, Pallas kernels: none -> 139 us  [body(): pl.pallas_call(kernel, out_shape=(jax.ShapeDtypeStruct((16, D), BF16), ja...]
    dot_general x9 -> x0, matrix products: 52 us -> none  [the longest x3 20.4 us: contract_rows(): lax.dot_general(left, right, (((0,), (0,)), ((), ())), preferred_element_...]
    unnamed x8 -> x11, local copies, waits for them, and re-layouts: 0.08 us -> 15.1 us
    convert_element_type x5 -> x0, other arithmetic: 10.9 us -> none  [the longest x1 2.56 us: body(): sum_d.astype(jnp.bfloat16)]
  transfers between devices with their start and end apart: 7 -> 0, of which waited for: 7 -> 0; matrix products, arithmetic and copies ran while one was open for 6% -> 0% of each run, Pallas kernels for 0% -> 0%
where the time goes in v1:
time: 159 us
  Pallas kernels  139 us (87%)
  local copies, waits for them, and re-layouts  19.7 us (12%)
    pallas_call x1, Pallas kernels, body(): pl.pallas_call(kernel, out_shape=(jax.ShapeDtypeStruct((16, D), BF16), ja...  139 us
    unnamed x11, local copies, waits for them, and re-layouts  15.1 us
    pallas_call x2, local copies, waits for them, and re-layouts, body(): pl.pallas_call(kernel, out_shape=(jax.ShapeDtypeStruct((16, D), BF16), ja...  4.52 us

profile of v1, /device:TPU:0, one launch (start us, length us, event | category | flops | bytes accessed | tf_op | source)
XLA Modules:
  0.0 159.1 jit_solution(15748767630439922988)
XLA Ops:
  0.6 6.4 %copy.10.wg = bf16[4096,448]{1,0:T(8,128)(2,1)} copy(bf16[4096,448]{0,1:T(8,128)(2,1)} %param.7) | data formatting | bytes 7340032 | tf_op args[2]
  7.1 6.5 %copy.11.wu = bf16[4096,448]{1,0:T(8,128)(2,1)} copy(bf16[4096,448]{0,1:T(8,128)(2,1)} %param.8) | data formatting | bytes 7340032 | tf_op args[3]
  13.5 138.7 %shard_map.92 = (bf16[16,4096]{1,0:T(8,128)(2,1)}, bf16[16,4096]{1,0:T(8,128)(2,1)}, bf16[1024,448]{1,0:T(8,128)(2,1)}, bf16[1024,448]{1,0:T(8,128)(2,1)}, bf16[448,1024]{1,0:T(8,128)(2,1)}) custom-call(bf16[16,4096]{1,0:T(8,128)(2,1)} %tok.1, bf16[16,4096]{1,0:T(8,128)(2,1)} %cot.1, bf16[4096,448]{1,0:T(8,128)(2,1)} %copy.10.wg, ...), custom_call_target="tpu_custom_call" | custom-call | flops 16999999488 | bytes 15000000 | tf_op jit(solution)/shard_map/pallas_call | solution.py:437
  152.3 0.0 copy-start.2
  152.3 0.0 copy-start.1
  152.3 0.0 copy-start
  152.3 2.3 %copy.12 = bf16[1024,448]{0,1:T(8,128)(2,1)} copy(bf16[1024,448]{1,0:T(8,128)(2,1)} %get-tuple-element.7) | data formatting | bytes 1835008 | tf_op jit(solution)/shard_map/pallas_call | solution.py:437
  154.6 2.2 %copy.13 = bf16[1024,448]{0,1:T(8,128)(2,1)} copy(bf16[1024,448]{1,0:T(8,128)(2,1)} %get-tuple-element.8) | data formatting | bytes 1835008 | tf_op jit(solution)/shard_map/pallas_call | solution.py:437
  156.8 0.0 copy-done.2
  156.8 0.7 copy.17
  157.5 0.0 copy-done.1
  157.5 0.7 copy.18
  158.1 0.0 copy-done
  158.1 0.9 copy.19
Async XLA Ops:
  152.3 4.6 %copy-start.2 = (bf16[16,4096]{1,0:T(8,128)(2,1)S(1)}, bf16[16,4096]{1,0:T(8,128)(2,1)}, u32[]{:S(2)}) copy-start(bf16[16,4096]{1,0:T(8,128)(2,1)} %get-tuple-element.15) | copy-start | bytes 393220
  152.3 5.2 %copy-start.1 = (bf16[16,4096]{1,0:T(8,128)(2,1)S(1)}, bf16[16,4096]{1,0:T(8,128)(2,1)}, u32[]{:S(2)}) copy-start(bf16[16,4096]{1,0:T(8,128)(2,1)} %get-tuple-element.16) | copy-start | bytes 393220
  152.3 5.9 %copy-start = (bf16[448,1024]{1,0:T(8,128)(2,1)S(1)}, bf16[448,1024]{1,0:T(8,128)(2,1)}, u32[]{:S(2)}) copy-start(bf16[448,1024]{1,0:T(8,128)(2,1)} %get-tuple-element.19) | copy-start | bytes 2752516

commit v2 on v1

--- a/solution.py
+++ b/solution.py
@@ -71,9 +71,10 @@
             )
             cp.start()
             loads.append(cp)
-    wloads = [pltpu.make_async_copy(wg, WG, ls.at[8]), pltpu.make_async_copy(wu, WU, ls.at[9])]
-    for q in range(4):
-        wloads.append(pltpu.make_async_copy(wd.at[:, pl.ds(q * Q, Q)], WD.at[q], ls.at[10 + q]))
+    wloads = []
+    for i, (ref, dst) in enumerate(((wg, WG), (wu, WU), (wd, WD))):
+        for q in range(4):
+            wloads.append(pltpu.make_async_copy(ref.at[:, pl.ds(q * Q, Q)], dst.at[q], ls.at[8 + i * 4 + q]))
     for cp in wloads:
         cp.start()
 
@@ -85,53 +86,65 @@
         pl.semaphore_signal(barrier, inc=1, device_id=p, device_id_type=MESH)
     pl.semaphore_wait(barrier, len(peers))
 
-    base = (0, 2, 4 + (1 - xl) * 2, 4 + xl * 2)
+    base = (0, 2, 4 + (1 - xl) * 2, 4 + (1 - xl) * 2, 4 + xl * 2)
+    cols = (pl.ds(0, Q), pl.ds(0, Q), pl.ds(0, 512), pl.ds(512, 512), pl.ds(0, Q))
 
     def blk(u, h, a, b):
-        return X.at[(base[u] + h,) + at(h, a, b)]
+        return X.at[(base[u] + h,) + at(h, a, b) + (slice(None), cols[u])]
 
     def sub(u, h, a, b, row):
-        return X.at[(base[u] + h,) + at(h, a, b) + (pl.ds(row, 16),)]
+        return X.at[(base[u] + h,) + at(h, a, b) + (pl.ds(row, 16), cols[u])]
 
     def gsend(u, i, ref, to):
         send(ref, ref, gs.at[u, i], gr.at[u, i], to)
 
     def g_start(u):
-        ref = X.at[pl.ds(base[u], 2), z, y, pl.ds(my_row, 16)]
+        ref = X.at[pl.ds(base[u], 2), z, y, pl.ds(my_row, 16), cols[u]]
         gsend(u, 0, ref, h_pair)
         for s, off in enumerate(OFFS):
             for h in range(2):
                 gsend(u, 1 + h * 6 + s, sub(u, h, me_a[h], me_b[h], my_row), peer(h, da=off))
+        g_near(u, my_row, 13, 8)
+
+    def g_near(u, row, i, step):
+        for h in range(2):
+            for d, off in enumerate((1, -1)):
+                gsend(u, i + h * step + d, sub(u, h, me_a[h], me_b[h], row), peer(h, db=off))
 
     def g_spread(u, s):
         for h in range(2):
-            a = me_a[h] if s == 0 else ring(me_a[h], -OFFS[s - 1])
+            a = ring(me_a[h], -OFFS[s - 1])
             for d, off in enumerate((1, -1)):
                 gsend(u, 13 + h * 8 + s * 2 + d, blk(u, h, a, me_b[h]), peer(h, db=off))
 
     def g_own(u):
-        arrived(X.at[pl.ds(base[u], 2), z, y, pl.ds(pair_row, 16)], gr.at[u, 0])
+        arrived(X.at[pl.ds(base[u], 2), z, y, pl.ds(pair_row, 16), cols[u]], gr.at[u, 0])
         for s, off in enumerate(OFFS):
             for h in range(2):
                 gsend(u, 4 + h * 6 + s, sub(u, h, me_a[h], me_b[h], pair_row), peer(h, da=off))
-        g_spread(u, 0)
-
-    def g_mid(u, s):
-        off = OFFS[s - 1]
-        for h in range(2):
-            a = ring(me_a[h], -off)
-            arrived(sub(u, h, a, me_b[h], my_row), gr.at[u, 1 + h * 6 + s - 1])
-            arrived(sub(u, h, a, me_b[h], pair_row), gr.at[u, 4 + h * 6 + s - 1])
-        g_spread(u, s)
-
-    def g_forward(u, s):
-        for h in range(2):
-            a = me_a[h] if s == 0 else ring(me_a[h], -OFFS[s - 1])
-            for d, off in enumerate((1, -1)):
-                b = ring(me_b[h], -off)
-                i = h * 8 + s * 2 + d
-                arrived(blk(u, h, a, b), gr.at[u, 13 + i])
-                gsend(u, 29 + i, sub(u, h, a, b, d * 16), peer(h, db=off))
+        g_near(u, pair_row, 45, 2)
+
+    def g_mid(u):
+        for s in (1, 2, 3):
+            for h in range(2):
+                a = ring(me_a[h], -OFFS[s - 1])
+                arrived(sub(u, h, a, me_b[h], my_row), gr.at[u, 1 + h * 6 + s - 1])
+                arrived(sub(u, h, a, me_b[h], pair_row), gr.at[u, 4 + h * 6 + s - 1])
+            g_spread(u, s)
+
+    def g_forward(u):
+        for s in range(4):
+            for h in range(2):
+                a = me_a[h] if s == 0 else ring(me_a[h], -OFFS[s - 1])
+                for d, off in enumerate((1, -1)):
+                    b = ring(me_b[h], -off)
+                    i = h * 8 + s * 2 + d
+                    if s == 0:
+                        arrived(sub(u, h, a, b, my_row), gr.at[u, 13 + i])
+                        arrived(sub(u, h, a, b, pair_row), gr.at[u, 45 + h * 2 + d])
+                    else:
+                        arrived(blk(u, h, a, b), gr.at[u, 13 + i])
+                    gsend(u, 29 + i, sub(u, h, a, b, d * 16), peer(h, db=off))
 
     def g_done(u):
         for s in range(4):
@@ -148,8 +161,8 @@
             def step(r, _):
                 x = rows_of(q, r)
                 rows = pl.ds(pl.multiple_of(r * 256, 256), 256)
-                g = mm(x, WG[pl.ds(q * Q, Q), :])
-                u = mm(x, WU[pl.ds(q * Q, Q), :])
+                g = mm_nt(x, WG[q])
+                u = mm_nt(x, WU[q])
                 if q == 0:
                     gate[rows, :] = g
                     up[rows, :] = u
@@ -196,7 +209,8 @@
         for h in range(2):
             def step(r, _):
                 rows = pl.ds(pl.multiple_of(r * 256, 256), 256)
-                v = mm_nt(rows_of(base[u] + h, r), WD[base[u] - 4 + h])
+                x = X[base[u] + h, pl.ds(2 * r, 2), :, :, cols[u]]
+                v = mm_nt(x.reshape(256, x.shape[-1]), WD[base[u] - 4 + h, :, cols[u]])
                 if first and h == 0:
                     dhid[rows, :] = v
                 else:
@@ -208,7 +222,7 @@
     def input_part(q):
         def step(r, _):
             rows = pl.ds(pl.multiple_of(r * 256, 256), 256)
-            v = mm_nt(dgate[rows, :], WG[pl.ds(q * Q, Q), :]) + mm_nt(dup[rows, :], WU[pl.ds(q * Q, Q), :])
+            v = mm(dgate[rows, :], WG[q]) + mm(dup[rows, :], WU[q])
             PS[4 + q, pl.ds(2 * r, 2)] = v.astype(BF16).reshape(2, 4, 32, Q)
             return 0
 
@@ -284,170 +298,185 @@
             q = (v % 2) * 2 + h
             OB[v // 2, :, q * Q:(q + 1) * Q] = (TO[v, h] + R3[v, h].astype(F32)).astype(BF16)
         if v % 2 == 1:
-            cp = pltpu.make_async_copy(OB.at[v // 2], (out, ig)[v // 2], ls.at[14 + v // 2])
+            cp = pltpu.make_async_copy(OB.at[v // 2], (out, ig)[v // 2], ls.at[20 + v // 2])
             cp.start()
             stores.append(cp)
 
     lhs, x0 = (hidT, dgT, duT), (4, 0, 0)
     jobs = {}
 
-    def w_part(j):
+    def w_part(j, n):
         arr, w = j % 3, (1 - xl) if j < 3 else xl
+        part = pl.ds(n * 512, 512)
         if j >= 2:
-            jobs[j - 2].wait_send()
-            started[:] = [cp for cp in started if cp is not jobs[j - 2]]
+            old = jobs[j - 2, n]
+            old.wait_send()
+            started[:] = [cp for cp in started if cp is not old]
 
         def step(k, _):
             quarter = w * 2 + jnp.where(k == 0, 1 - c, c)
             slot = jnp.where(k == 0, 6 + j % 2, j)
-            for n in range(2):
-                xb = X[x0[arr] + quarter, :, :, :, n * 512:(n + 1) * 512].reshape(T, 512)
-                WB[slot, :, n * 512:(n + 1) * 512] = mm(lhs[arr][...], xb).astype(BF16)
+            xb = X[x0[arr] + quarter, :, :, :, part].reshape(T, 512)
+            WB[slot, :, part] = mm(lhs[arr][...], xb).astype(BF16)
             return 0
 
         lax.fori_loop(0, 2, step, 0)
-        jobs[j] = send(WB.at[6 + j % 2], CR.at[j], cs.at[j], cr.at[j], core_pair)
-
-    def w_cross(j):
-        arrived(CR.at[j], cr.at[j])
+        jobs[j, n] = send(
+            WB.at[6 + j % 2, :, part], CR.at[j, :, part], cs.at[j, n], cr.at[j, n], core_pair
+        )
+
+    def w_cross(j, n):
+        part = pl.ds(n * 512, 512)
+        arrived(CR.at[j, :, part], cr.at[j, n])
 
         def step(r, _):
             rows = pl.ds(pl.multiple_of(r * 64, 64), 64)
-            WB[j, rows, :] = (WB[j, rows, :].astype(F32) + CR[j, rows, :].astype(F32)).astype(BF16)
+            WB[j, rows, part] = (WB[j, rows, part].astype(F32) + CR[j, rows, part].astype(F32)).astype(BF16)
             return 0
 
         lax.fori_loop(0, 7, step, 0)
-        send(WB.at[j], XR.at[j], xs.at[j], xr.at[j], x_pair)
-
-    def w_finish(arr):
+        send(WB.at[j, :, part], XR.at[j, :, part], xs.at[j, n], xr.at[j, n], x_pair)
+
+    def w_finish(arr, n):
         j = 3 + arr
-        arrived(CR.at[j], cr.at[j])
-        arrived(XR.at[arr], xr.at[arr])
-        if arr == 0:
-            def step(r, _):
-                rows = pl.ds(pl.multiple_of(r * 64, 64), 64)
-                v = WB[j, rows, :].astype(F32) + CR[j, rows, :].astype(F32) + XR[arr, rows, :].astype(F32)
-                WB[j, rows, :] = v.astype(BF16)
-                return 0
-
-            lax.fori_loop(0, 7, step, 0)
-            cp = pltpu.make_async_copy(WB.at[j], dg, ls.at[16])
-        else:
-            buf = (WG, WU)[arr - 1]
-            for n in range(8):
-                cols = slice(n * 128, (n + 1) * 128)
-                v = WB[j, :, cols].astype(F32) + CR[j, :, cols].astype(F32) + XR[arr, :, cols].astype(F32)
-                buf[cols, :] = v.T.astype(BF16)
-            cp = pltpu.make_async_copy(buf.at[pl.ds(0, Q)], (gg, ug)[arr - 1], ls.at[16 + arr])
+        part = pl.ds(n * 512, 512)
+        arrived(CR.at[j, :, part], cr.at[j, n])
+        arrived(XR.at[arr, :, part], xr.at[arr, n])
+
+        def step(r, _):
+            rows = pl.ds(pl.multiple_of(r * 64, 64), 64)
+            v = WB[j, rows, part].astype(F32) + CR[j, rows, part].astype(F32) + XR[arr, rows, part].astype(F32)
+            WB[j, rows, part] = v.astype(BF16)
+            return 0
+
+        lax.fori_loop(0, 7, step, 0)
+        cp = pltpu.make_async_copy(WB.at[j, :, part], (dg, gg, ug)[arr].at[:, part], ls.at[22 + arr * 2 + n])
         cp.start()
         stores.append(cp)
 
     for cp in loads:
         cp.wait()
     g_start(0)
+    g_start(1)
     g_own(0)
-    g_start(1)
-    for s in (1, 2, 3):
-        g_mid(0, s)
-    g_forward(0, 0)
     g_own(1)
-    for s in (1, 2, 3):
-        g_forward(0, s)
+    g_mid(0)
+    g_forward(0)
     g_start(2)
-    for s in (1, 2, 3):
-        g_mid(1, s)
+    g_mid(1)
+    g_own(2)
     g_done(0)
     for cp in wloads:
         cp.wait()
     gate_up(0)
-    g_own(2)
-    for s in range(4):
-        g_forward(1, s)
+    g_forward(1)
+    g_mid(2)
     g_start(3)
-    for s in (1, 2, 3):
-        g_mid(2, s)
     g_done(1)
+    g_own(3)
     gate_up(1)
-    g_own(3)
-    for s in range(4):
-        g_forward(2, s)
+    g_forward(2)
+    g_mid(3)
+    g_start(4)
     hidden()
-    for s in (1, 2, 3):
-        g_mid(3, s)
     transpose(hid, hidT)
     g_done(2)
-    w_part(0)
-    for s in range(4):
-        g_forward(3, s)
-    w_cross(0)
+    w_part(0, 0)
+    g_own(4)
+    g_forward(3)
+    w_cross(0, 0)
+    g_mid(4)
     output_part(0)
+    g_done(3)
+    w_part(0, 1)
     output_part(1)
+    w_cross(0, 1)
+    g_forward(4)
     s_first(0)
     output_part(2)
+    dhidden_part(2, True)
+    dhidden_part(3, False)
     output_part(3)
     s_first(1)
-    dhidden_part(2, True)
-    g_done(3)
-    dhidden_part(3, False)
+    g_done(4)
+    dhidden_part(4, False)
     backward()
     transpose(dgate, dgT)
-    w_part(1)
+    w_part(1, 0)
+    w_part(1, 1)
+    w_cross(1, 0)
     transpose(dup, duT)
+    w_cross(1, 1)
     s_join(0)
-    w_part(2)
-    w_cross(1)
+    w_part(2, 0)
+    w_part(2, 1)
+    w_cross(2, 0)
     s_join(1)
+    w_cross(2, 1)
     input_part(0)
     input_part(1)
-    w_cross(2)
     s_first(2)
     s_second(0)
     input_part(2)
     input_part(3)
     s_first(3)
     s_second(1)
-    w_part(3)
     s_join(2)
+    w_part(3, 0)
+    w_part(3, 1)
     s_third(0)
-    w_part(4)
     s_join(3)
     s_third(1)
-    w_part(5)
+    w_part(4, 0)
+    w_part(4, 1)
+    s_second(2)
+    w_part(5, 0)
+    w_part(5, 1)
+    s_second(3)
+    w_finish(0, 0)
+    w_finish(0, 1)
+    s_third(2)
+    s_third(3)
     s_finish(0)
     s_finish(1)
-    s_second(2)
-    w_finish(0)
-    s_second(3)
-    s_third(2)
-    s_third(3)
+    w_finish(1, 0)
+    w_finish(1, 1)
     s_finish(2)
     s_finish(3)
-    w_finish(1)
-    w_finish(2)
+    w_finish(2, 0)
+    w_finish(2, 1)
     for cp in started:
         cp.wait_send()
     for cp in stores:
         cp.wait()
 
 
+def store(*refs):
+    sems = refs[15]
+    into = [pltpu.make_async_copy(refs[i], refs[10 + i], sems.at[i]) for i in range(5)]
+    back = [pltpu.make_async_copy(refs[10 + i], refs[5 + i], sems.at[5 + i]) for i in range(5)]
+    for cp in into:
+        cp.start()
+    for a, b in zip(into, back):
+        a.wait()
+        b.start()
+    for cp in back:
+        cp.wait()
+
+
 def body(tokens, cotangent, gate_weight, up_weight, down_weight):
     any_spec = pl.BlockSpec(memory_space=pl.ANY)
     vm, dma = pltpu.VMEM, pltpu.SemaphoreType.DMA
     blocks = (4, 4, 32, Q)
-    return pl.pallas_call(
+    shapes = [jax.ShapeDtypeStruct((16, D), BF16)] * 2 + [jax.ShapeDtypeStruct((H, Q), BF16)] * 3
+    results = pl.pallas_call(
         kernel,
-        out_shape=(
-            jax.ShapeDtypeStruct((16, D), BF16),
-            jax.ShapeDtypeStruct((16, D), BF16),
-            jax.ShapeDtypeStruct((Q, H), BF16),
-            jax.ShapeDtypeStruct((Q, H), BF16),
-            jax.ShapeDtypeStruct((H, Q), BF16),
-        ),
+        out_shape=shapes,
         in_specs=[any_spec] * 5,
         out_specs=[any_spec] * 5,
         scratch_shapes=[
             vm((8,) + blocks, BF16),
-            vm((D, H), BF16), vm((D, H), BF16), vm((4, H, Q), BF16),
+            vm((4, H, Q), BF16), vm((4, H, Q), BF16), vm((4, H, Q), BF16),
             vm((T, H), F32), vm((T, H), F32), vm((T, H), F32),
             vm((T, H), BF16), vm((T, H), BF16), vm((T, H), BF16),
             vm((H, T), BF16), vm((H, T), BF16), vm((H, T), BF16),
@@ -459,14 +488,22 @@
             vm((4, 2, 16, Q), F32), vm((4, 2, 32, Q), F32),
             vm((2, 16, D), BF16),
             vm((8, H, Q), BF16), vm((6, H, Q), BF16), vm((3, H, Q), BF16),
-            dma((19,)), dma((4, 45)), dma((4, 45)), dma((4, 19)), dma((4, 19)),
-            dma((6,)), dma((6,)), dma((3,)), dma((3,)),
+            dma((28,)), dma((5, 49)), dma((5, 49)), dma((4, 19)), dma((4, 19)),
+            dma((6, 2)), dma((6, 2)), dma((3, 2)), dma((3, 2)),
         ],
         compiler_params=pltpu.CompilerParams(
             collective_id=0, has_side_effects=True, vmem_limit_bytes=62 * 1024 * 1024
         ),
         cost_estimate=pl.CostEstimate(flops=17_000_000_000, bytes_accessed=15_000_000, transcendentals=460_000),
-    )(tokens, cotangent, gate_weight, up_weight, down_weight)
+    )(tokens, cotangent, gate_weight.T, up_weight.T, down_weight)
+    output, input_grad, gate_grad, up_grad, down_grad = pl.pallas_call(
+        store,
+        out_shape=shapes,
+        in_specs=[any_spec] * 5,
+        out_specs=[any_spec] * 5,
+        scratch_shapes=[vm(x.shape, BF16) for x in shapes] + [dma((10,))],
+    )(*results)
+    return output, input_grad, gate_grad.T, up_grad.T, down_grad
 
 
 def solution(mesh):

time: 159 us -> 125 us (0.79)
  local copies, waits for them, and re-layouts: 19.7 us -> 0 us
  Pallas kernels: 139 us -> 123 us
    pallas_call x1 -> x2, Pallas kernels: 139 us -> 123 us  [the longest x1 120 us: body(): pl.pallas_call(kernel, out_shape=shapes, in_specs=[any_spec] * 5, out_spe...]
    unnamed x11 -> x0, local copies, waits for them, and re-layouts: 15.1 us -> none
    pallas_call x2 -> x0, local copies, waits for them, and re-layouts: 4.52 us -> none  [body(): pl.pallas_call(kernel, out_shape=(jax.ShapeDtypeStruct((16, D), BF16), ja...]
where the time goes in v2:
time: 125 us; the launch traced here: 124 us
  Pallas kernels  123 us (98%)
    pallas_call x1, Pallas kernels, body(): pl.pallas_call(kernel, out_shape=shapes, in_specs=[any_spec] * 5, out_spe...  120 us
    pallas_call x1, Pallas kernels, body(): pl.pallas_call(store, out_shape=shapes, in_specs=[any_spec] * 5, out_spec...  2.98 us

profile of v2, /device:TPU:0, one launch (start us, length us, event | category | flops | bytes accessed | tf_op | source)
XLA Modules:
  0.0 124.3 jit_solution(4613239547263677565)
XLA Ops:
  0.6 120.5 %shard_map.92 = (bf16[16,4096]{1,0:T(8,128)(2,1)}, bf16[16,4096]{1,0:T(8,128)(2,1)}, bf16[448,1024]{1,0:T(8,128)(2,1)}, bf16[448,1024]{1,0:T(8,128)(2,1)}, bf16[448,1024]{1,0:T(8,128)(2,1)}) custom-call(bf16[16,4096]{1,0:T(8,128)(2,1)} %tok.1, bf16[16,4096]{1,0:T(8,128)(2,1)} %cot.1, bf16[448,4096]{1,0:T(8,128)(2,1)} %bitcast.4, bf16[448,4096]{1,0:T(8,128)(2,1)} %bitcast.5, ...), custom_call_target="tpu_custom_call" | custom-call | flops 16999999488 | bytes 15000000 | tf_op jit(solution)/shard_map/pallas_call | solution.py:472
  121.1 3.0 %shard_map.93 = (bf16[16,4096]{1,0:T(8,128)(2,1)}, bf16[16,4096]{1,0:T(8,128)(2,1)}, bf16[448,1024]{1,0:T(8,128)(2,1)}, bf16[448,1024]{1,0:T(8,128)(2,1)}, bf16[448,1024]{1,0:T(8,128)(2,1)}) custom-call(bf16[16,4096]{1,0:T(8,128)(2,1)} %get-tuple-element.15.refs_0_, bf16[16,4096]{1,0:T(8,128)(2,1)} %get-tuple-element.16.refs_1_, ...), custom_call_target="tpu_custom_call" | custom-call | tf_op jit(solution)/shard_map/pallas_call | solution.py:499

commit v3 on v2

--- a/solution.py
+++ b/solution.py
@@ -62,6 +62,13 @@
 
     def arrived(ref, r):
         pltpu.make_async_copy(ref, ref, r).wait()
+
+    barrier = pltpu.get_barrier_semaphore()
+    peers = [x_pair, core_pair, h_pair]
+    for off in OFFS:
+        peers += [dev(ring(z, off), y), dev(z, ring(y, off))]
+    for p in peers:
+        pl.semaphore_signal(barrier, inc=1, device_id=p, device_id_type=MESH)
 
     loads = []
     for arr, ref in enumerate((tok, cot)):
@@ -78,12 +85,6 @@
     for cp in wloads:
         cp.start()
 
-    barrier = pltpu.get_barrier_semaphore()
-    peers = [x_pair, core_pair, h_pair]
-    for off in OFFS:
-        peers += [dev(ring(z, off), y), dev(z, ring(y, off))]
-    for p in peers:
-        pl.semaphore_signal(barrier, inc=1, device_id=p, device_id_type=MESH)
     pl.semaphore_wait(barrier, len(peers))
 
     base = (0, 2, 4 + (1 - xl) * 2, 4 + (1 - xl) * 2, 4 + xl * 2)
@@ -98,9 +99,12 @@
     def gsend(u, i, ref, to):
         send(ref, ref, gs.at[u, i], gr.at[u, i], to)
 
+    LATE = (0,)
+
+    def g_pair(u):
+        gsend(u, 0, X.at[pl.ds(base[u], 2), z, y, pl.ds(my_row, 16), cols[u]], h_pair)
+
     def g_start(u):
-        ref = X.at[pl.ds(base[u], 2), z, y, pl.ds(my_row, 16), cols[u]]
-        gsend(u, 0, ref, h_pair)
         for s, off in enumerate(OFFS):
             for h in range(2):
                 gsend(u, 1 + h * 6 + s, sub(u, h, me_a[h], me_b[h], my_row), peer(h, da=off))
@@ -110,12 +114,6 @@
         for h in range(2):
             for d, off in enumerate((1, -1)):
                 gsend(u, i + h * step + d, sub(u, h, me_a[h], me_b[h], row), peer(h, db=off))
-
-    def g_spread(u, s):
-        for h in range(2):
-            a = ring(me_a[h], -OFFS[s - 1])
-            for d, off in enumerate((1, -1)):
-                gsend(u, 13 + h * 8 + s * 2 + d, blk(u, h, a, me_b[h]), peer(h, db=off))
 
     def g_own(u):
         arrived(X.at[pl.ds(base[u], 2), z, y, pl.ds(pair_row, 16), cols[u]], gr.at[u, 0])
@@ -124,34 +122,70 @@
                 gsend(u, 4 + h * 6 + s, sub(u, h, me_a[h], me_b[h], pair_row), peer(h, da=off))
         g_near(u, pair_row, 45, 2)
 
+    def g_part(u, h, s, b):
+        a = me_a[h] if s == 0 else ring(me_a[h], -OFFS[s - 1])
+        return sub(u, h, a, b, my_row) if u in LATE else blk(u, h, a, b)
+
     def g_mid(u):
         for s in (1, 2, 3):
             for h in range(2):
                 a = ring(me_a[h], -OFFS[s - 1])
-                arrived(sub(u, h, a, me_b[h], my_row), gr.at[u, 1 + h * 6 + s - 1])
-                arrived(sub(u, h, a, me_b[h], pair_row), gr.at[u, 4 + h * 6 + s - 1])
-            g_spread(u, s)
+                mine = sub(u, h, a, me_b[h], my_row)
+                arrived(mine, gr.at[u, s + h * 6])
+                if u not in LATE:
+                    arrived(sub(u, h, a, me_b[h], pair_row), gr.at[u, 3 + s + h * 6])
+                for d, off in enumerate((1, -1)):
+                    gsend(u, 13 + h * 8 + s * 2 + d, g_part(u, h, s, me_b[h]), peer(h, db=off))
+        if u in LATE:
+            g_swap(u, 0)
+
+    def plane(u, h, b, row):
+        tail = (pl.ds(row, 16), cols[u])
+        i = base[u] + h
+        return X.at[(i, b, slice(None)) + tail] if h == 0 else X.at[(i, slice(None), b) + tail]
+
+    def g_swap(u, stage):
+        for h in range(2):
+            for k in ((0,), (1, 2), (3,))[stage]:
+                gsend(u, 45 + h * 4 + k, plane(u, h, ring(me_b[h], (0, 1, -1, 2)[k]), my_row), h_pair)
 
     def g_forward(u):
         for s in range(4):
             for h in range(2):
-                a = me_a[h] if s == 0 else ring(me_a[h], -OFFS[s - 1])
                 for d, off in enumerate((1, -1)):
                     b = ring(me_b[h], -off)
                     i = h * 8 + s * 2 + d
-                    if s == 0:
-                        arrived(sub(u, h, a, b, my_row), gr.at[u, 13 + i])
-                        arrived(sub(u, h, a, b, pair_row), gr.at[u, 45 + h * 2 + d])
+                    if s == 0 and u not in LATE:
+                        arrived(sub(u, h, me_a[h], b, my_row), gr.at[u, 13 + i])
+                        arrived(sub(u, h, me_a[h], b, pair_row), gr.at[u, 45 + h * 2 + d])
                     else:
-                        arrived(blk(u, h, a, b), gr.at[u, 13 + i])
-                    gsend(u, 29 + i, sub(u, h, a, b, d * 16), peer(h, db=off))
+                        arrived(g_part(u, h, s, b), gr.at[u, 13 + i])
+                    if u not in LATE:
+                        a = me_a[h] if s == 0 else ring(me_a[h], -OFFS[s - 1])
+                        gsend(u, 29 + i, sub(u, h, a, b, d * 16), peer(h, db=off))
+                    elif s // 2 == d:
+                        gsend(u, 29 + i, g_part(u, h, s, b), peer(h, db=off))
+        if u in LATE:
+            g_swap(u, 1)
 
     def g_done(u):
         for s in range(4):
             for h in range(2):
-                a = me_a[h] if s == 0 else ring(me_a[h], -OFFS[s - 1])
+                b = ring(me_b[h], 2)
                 for d in range(2):
-                    arrived(sub(u, h, a, ring(me_b[h], 2), d * 16), gr.at[u, 29 + h * 8 + s * 2 + d])
+                    i = 29 + h * 8 + s * 2 + d
+                    if u not in LATE:
+                        a = me_a[h] if s == 0 else ring(me_a[h], -OFFS[s - 1])
+                        arrived(sub(u, h, a, b, d * 16), gr.at[u, i])
+                    elif s // 2 == d:
+                        arrived(g_part(u, h, s, b), gr.at[u, i])
+        if u in LATE:
+            g_swap(u, 2)
+
+    def g_swapped(u):
+        for h in range(2):
+            for k in range(4):
+                arrived(plane(u, h, ring(me_b[h], (0, 1, -1, 2)[k]), pair_row), gr.at[u, 45 + h * 4 + k])
 
     def rows_of(i, r):
         return X[i, pl.ds(2 * r, 2)].reshape(256, Q)
@@ -163,7 +197,7 @@
                 rows = pl.ds(pl.multiple_of(r * 256, 256), 256)
                 g = mm_nt(x, WG[q])
                 u = mm_nt(x, WU[q])
-                if q == 0:
+                if q == 2:
                     gate[rows, :] = g
                     up[rows, :] = u
                 else:
@@ -182,16 +216,24 @@
 
         lax.fori_loop(0, 16, step, 0)
 
-    def backward():
+    def factors():
         def step(r, _):
             rows = pl.ds(pl.multiple_of(r * 32, 32), 32)
-            g, dh = gate[rows, :], dhid[rows, :]
+            g = gate[rows, :]
             sig = jax.nn.sigmoid(g)
-            dgate[rows, :] = (dh * up[rows, :] * sig * (1.0 + g * (1.0 - sig))).astype(BF16)
-            dup[rows, :] = (dh * (g * sig)).astype(BF16)
+            gate[rows, :] = up[rows, :] * sig * (1.0 + g * (1.0 - sig))
+            up[rows, :] = g * sig
             return 0
 
         lax.fori_loop(0, 16, step, 0)
+
+    def backward(dst, factor):
+        def step(r, _):
+            rows = pl.ds(pl.multiple_of(r * 64, 64), 64)
+            dst[rows, :] = (dhid[rows, :] * factor[rows, :]).astype(BF16)
+            return 0
+
+        lax.fori_loop(0, 8, step, 0)
 
     def transpose(src, dst):
         for r in range(4):
@@ -356,9 +398,12 @@
 
     for cp in loads:
         cp.wait()
+    g_pair(1)
     g_start(0)
     g_start(1)
-    g_own(0)
+    g_pair(2)
+    g_pair(3)
+    g_pair(4)
     g_own(1)
     g_mid(0)
     g_forward(0)
@@ -368,7 +413,6 @@
     g_done(0)
     for cp in wloads:
         cp.wait()
-    gate_up(0)
     g_forward(1)
     g_mid(2)
     g_start(3)
@@ -378,6 +422,8 @@
     g_forward(2)
     g_mid(3)
     g_start(4)
+    g_swapped(0)
+    gate_up(0)
     hidden()
     transpose(hid, hidT)
     g_done(2)
@@ -391,6 +437,7 @@
     w_part(0, 1)
     output_part(1)
     w_cross(0, 1)
+    factors()
     g_forward(4)
     s_first(0)
     output_part(2)
@@ -400,50 +447,51 @@
     s_first(1)
     g_done(4)
     dhidden_part(4, False)
-    backward()
+    backward(dgate, gate)
     transpose(dgate, dgT)
     w_part(1, 0)
     w_part(1, 1)
+    backward(dup, up)
     w_cross(1, 0)
-    transpose(dup, duT)
     w_cross(1, 1)
     s_join(0)
-    w_part(2, 0)
-    w_part(2, 1)
-    w_cross(2, 0)
-    s_join(1)
-    w_cross(2, 1)
     input_part(0)
     input_part(1)
     s_first(2)
+    transpose(dup, duT)
+    w_part(2, 0)
+    s_join(1)
+    w_part(2, 1)
+    w_cross(2, 0)
     s_second(0)
     input_part(2)
     input_part(3)
     s_first(3)
     s_second(1)
     s_join(2)
+    s_third(0)
     w_part(3, 0)
     w_part(3, 1)
-    s_third(0)
     s_join(3)
     s_third(1)
+    w_cross(2, 1)
     w_part(4, 0)
     w_part(4, 1)
     s_second(2)
     w_part(5, 0)
     w_part(5, 1)
-    s_second(3)
     w_finish(0, 0)
     w_finish(0, 1)
     s_third(2)
-    s_third(3)
+    s_second(3)
     s_finish(0)
     s_finish(1)
     w_finish(1, 0)
+    s_third(3)
     w_finish(1, 1)
     s_finish(2)
+    w_finish(2, 0)
     s_finish(3)
-    w_finish(2, 0)
     w_finish(2, 1)
     for cp in started:
         cp.wait_send()
@@ -488,7 +536,7 @@
             vm((4, 2, 16, Q), F32), vm((4, 2, 32, Q), F32),
             vm((2, 16, D), BF16),
             vm((8, H, Q), BF16), vm((6, H, Q), BF16), vm((3, H, Q), BF16),
-            dma((28,)), dma((5, 49)), dma((5, 49)), dma((4, 19)), dma((4, 19)),
+            dma((28,)), dma((5, 53)), dma((5, 53)), dma((4, 19)), dma((4, 19)),
             dma((6, 2)), dma((6, 2)), dma((3, 2)), dma((3, 2)),
         ],
         compiler_params=pltpu.CompilerParams(

time: 125 us -> 120 us (0.960)
  Pallas kernels: 123 us -> 118 us
    pallas_call x1, Pallas kernels: 120 us -> 115 us  [body(): pl.pallas_call(kernel, out_shape=shapes, in_specs=[any_spec] * 5, out_spe...]
where the time goes in v3:
time: 120 us; the launch traced here: 119 us
  Pallas kernels  118 us (98%)
    pallas_call x1, Pallas kernels, body(): pl.pallas_call(kernel, out_shape=shapes, in_specs=[any_spec] * 5, out_spe...  115 us
    pallas_call x1, Pallas kernels, body(): pl.pallas_call(store, out_shape=shapes, in_specs=[any_spec] * 5, out_spec...  2.98 us

profile of v3, /device:TPU:0, one launch (start us, length us, event | category | flops | bytes accessed | tf_op | source)
XLA Modules:
  0.0 118.5 jit_solution(3616182870958229534)
XLA Ops:
  0.6 114.8 %shard_map.92 = (bf16[16,4096]{1,0:T(8,128)(2,1)}, bf16[16,4096]{1,0:T(8,128)(2,1)}, bf16[448,1024]{1,0:T(8,128)(2,1)}, bf16[448,1024]{1,0:T(8,128)(2,1)}, bf16[448,1024]{1,0:T(8,128)(2,1)}) custom-call(bf16[16,4096]{1,0:T(8,128)(2,1)} %tok.1, bf16[16,4096]{1,0:T(8,128)(2,1)} %cot.1, bf16[448,4096]{1,0:T(8,128)(2,1)} %bitcast.4, bf16[448,4096]{1,0:T(8,128)(2,1)} %bitcast.5, ...), custom_call_target="tpu_custom_call" | custom-call | flops 16999999488 | bytes 15000000 | tf_op jit(solution)/shard_map/pallas_call | solution.py:520
  115.4 3.0 %shard_map.93 = (bf16[16,4096]{1,0:T(8,128)(2,1)}, bf16[16,4096]{1,0:T(8,128)(2,1)}, bf16[448,1024]{1,0:T(8,128)(2,1)}, bf16[448,1024]{1,0:T(8,128)(2,1)}, bf16[448,1024]{1,0:T(8,128)(2,1)}) custom-call(bf16[16,4096]{1,0:T(8,128)(2,1)} %get-tuple-element.15.refs_0_, bf16[16,4096]{1,0:T(8,128)(2,1)} %get-tuple-element.16.refs_1_, ...), custom_call_target="tpu_custom_call" | custom-call | tf_op jit(solution)/shard_map/pallas_call | solution.py:547

commit v4 on v3

--- a/solution.py
+++ b/solution.py
@@ -8,6 +8,7 @@
 MESH = pl.DeviceIdType.MESH
 BF16, F32 = jnp.bfloat16, jnp.float32
 T, D, H, Q = 512, 4096, 448, 1024
+PARTS = (pl.ds(0, 512), pl.ds(512, 512))
 
 
 def mm(a, b):
@@ -88,7 +89,7 @@
     pl.semaphore_wait(barrier, len(peers))
 
     base = (0, 2, 4 + (1 - xl) * 2, 4 + (1 - xl) * 2, 4 + xl * 2)
-    cols = (pl.ds(0, Q), pl.ds(0, Q), pl.ds(0, 512), pl.ds(512, 512), pl.ds(0, Q))
+    cols = (pl.ds(0, Q), pl.ds(0, Q), *PARTS, pl.ds(0, Q))
 
     def blk(u, h, a, b):
         return X.at[(base[u] + h,) + at(h, a, b) + (slice(None), cols[u])]
@@ -100,12 +101,13 @@
         send(ref, ref, gs.at[u, i], gr.at[u, i], to)
 
     LATE = (0,)
+    RELAY = (1,)
 
     def g_pair(u):
         gsend(u, 0, X.at[pl.ds(base[u], 2), z, y, pl.ds(my_row, 16), cols[u]], h_pair)
 
     def g_start(u):
-        for s, off in enumerate(OFFS):
+        for s, off in enumerate(OFFS[:2] if u in RELAY else OFFS):
             for h in range(2):
                 gsend(u, 1 + h * 6 + s, sub(u, h, me_a[h], me_b[h], my_row), peer(h, da=off))
         g_near(u, my_row, 13, 8)
@@ -117,22 +119,33 @@
 
     def g_own(u):
         arrived(X.at[pl.ds(base[u], 2), z, y, pl.ds(pair_row, 16), cols[u]], gr.at[u, 0])
-        for s, off in enumerate(OFFS):
+        for s, off in enumerate(OFFS[:2] if u in RELAY else OFFS):
             for h in range(2):
                 gsend(u, 4 + h * 6 + s, sub(u, h, me_a[h], me_b[h], pair_row), peer(h, da=off))
         g_near(u, pair_row, 45, 2)
 
+    def g_relay(u):
+        for h in range(2):
+            low, high = ring(me_a[h], -1), ring(me_a[h], 1)
+            ref = sub(u, h, low, me_b[h], my_row)
+            arrived(ref, gr.at[u, 1 + h * 6])
+            gsend(u, 3 + h * 6, ref, peer(h, da=1))
+            ref = sub(u, h, high, me_b[h], pair_row)
+            arrived(ref, gr.at[u, 5 + h * 6])
+            gsend(u, 6 + h * 6, ref, peer(h, da=-1))
+
     def g_part(u, h, s, b):
         a = me_a[h] if s == 0 else ring(me_a[h], -OFFS[s - 1])
         return sub(u, h, a, b, my_row) if u in LATE else blk(u, h, a, b)
 
-    def g_mid(u):
-        for s in (1, 2, 3):
+    def g_mid(u, sides=(1, 2, 3)):
+        for s in sides:
             for h in range(2):
                 a = ring(me_a[h], -OFFS[s - 1])
                 mine = sub(u, h, a, me_b[h], my_row)
-                arrived(mine, gr.at[u, s + h * 6])
-                if u not in LATE:
+                if u not in RELAY or s != 1:
+                    arrived(mine, gr.at[u, s + h * 6])
+                if u not in LATE and (u not in RELAY or s != 2):
                     arrived(sub(u, h, a, me_b[h], pair_row), gr.at[u, 3 + s + h * 6])
                 for d, off in enumerate((1, -1)):
                     gsend(u, 13 + h * 8 + s * 2 + d, g_part(u, h, s, me_b[h]), peer(h, db=off))
@@ -182,30 +195,28 @@
         if u in LATE:
             g_swap(u, 2)
 
-    def g_swapped(u):
-        for h in range(2):
-            for k in range(4):
-                arrived(plane(u, h, ring(me_b[h], (0, 1, -1, 2)[k]), pair_row), gr.at[u, 45 + h * 4 + k])
+    def g_swapped(u, h):
+        for k in range(4):
+            arrived(plane(u, h, ring(me_b[h], (0, 1, -1, 2)[k]), pair_row), gr.at[u, 45 + h * 4 + k])
 
     def rows_of(i, r):
         return X[i, pl.ds(2 * r, 2)].reshape(256, Q)
 
-    def gate_up(w):
-        for q in (2 * w, 2 * w + 1):
-            def step(r, _):
-                x = rows_of(q, r)
-                rows = pl.ds(pl.multiple_of(r * 256, 256), 256)
-                g = mm_nt(x, WG[q])
-                u = mm_nt(x, WU[q])
-                if q == 2:
-                    gate[rows, :] = g
-                    up[rows, :] = u
-                else:
-                    gate[rows, :] += g
-                    up[rows, :] += u
-                return 0
-
-            lax.fori_loop(0, 2, step, 0)
+    def gate_up(q, first=False):
+        def step(r, _):
+            x = rows_of(q, r)
+            rows = pl.ds(pl.multiple_of(r * 256, 256), 256)
+            g = mm_nt(x, WG[q])
+            u = mm_nt(x, WU[q])
+            if first:
+                gate[rows, :] = g
+                up[rows, :] = u
+            else:
+                gate[rows, :] += g
+                up[rows, :] += u
+            return 0
+
+        lax.fori_loop(0, 2, step, 0)
 
     def hidden():
         def step(r, _):
@@ -349,26 +360,24 @@
 
     def w_part(j, n):
         arr, w = j % 3, (1 - xl) if j < 3 else xl
-        part = pl.ds(n * 512, 512)
+        part = PARTS[n]
         if j >= 2:
             old = jobs[j - 2, n]
             old.wait_send()
             started[:] = [cp for cp in started if cp is not old]
 
-        def step(k, _):
-            quarter = w * 2 + jnp.where(k == 0, 1 - c, c)
-            slot = jnp.where(k == 0, 6 + j % 2, j)
-            xb = X[x0[arr] + quarter, :, :, :, part].reshape(T, 512)
+        for k in range(2):
+            quarter = w * 2 + ((1 - c), c)[k]
+            slot = (6 + j % 2, j)[k]
+            xb = X[x0[arr] + quarter, :, :, :, part].reshape(T, part.size)
             WB[slot, :, part] = mm(lhs[arr][...], xb).astype(BF16)
-            return 0
-
-        lax.fori_loop(0, 2, step, 0)
-        jobs[j, n] = send(
-            WB.at[6 + j % 2, :, part], CR.at[j, :, part], cs.at[j, n], cr.at[j, n], core_pair
-        )
+            if k == 0:
+                jobs[j, n] = send(
+                    WB.at[slot, :, part], CR.at[j, :, part], cs.at[j, n], cr.at[j, n], core_pair
+                )
 
     def w_cross(j, n):
-        part = pl.ds(n * 512, 512)
+        part = PARTS[n]
         arrived(CR.at[j, :, part], cr.at[j, n])
 
         def step(r, _):
@@ -381,7 +390,7 @@
 
     def w_finish(arr, n):
         j = 3 + arr
-        part = pl.ds(n * 512, 512)
+        part = PARTS[n]
         arrived(CR.at[j, :, part], cr.at[j, n])
         arrived(XR.at[arr, :, part], xr.at[arr, n])
 
@@ -407,6 +416,7 @@
     g_own(1)
     g_mid(0)
     g_forward(0)
+    g_relay(1)
     g_start(2)
     g_mid(1)
     g_own(2)
@@ -418,27 +428,31 @@
     g_start(3)
     g_done(1)
     g_own(3)
-    gate_up(1)
+    gate_up(2, True)
+    gate_up(3)
     g_forward(2)
     g_mid(3)
     g_start(4)
-    g_swapped(0)
+    g_swapped(0, 0)
     gate_up(0)
+    g_own(4)
+    g_swapped(0, 1)
+    gate_up(1)
     hidden()
     transpose(hid, hidT)
     g_done(2)
     w_part(0, 0)
-    g_own(4)
     g_forward(3)
+    g_mid(4, (1, ))
     w_cross(0, 0)
-    g_mid(4)
-    output_part(0)
+    g_mid(4, (2, 3))
     g_done(3)
     w_part(0, 1)
+    output_part(0)
+    w_cross(0, 1)
     output_part(1)
-    w_cross(0, 1)
+    g_forward(4)
     factors()
-    g_forward(4)
     s_first(0)
     output_part(2)
     dhidden_part(2, True)

time: 120 us -> 120 us (level)
  no operation moved by 1% of the time
where the time goes in v4:
time: 120 us; the launch traced here: 119 us
  Pallas kernels  119 us (99%)
    pallas_call x1, Pallas kernels, body(): pl.pallas_call(kernel, out_shape=shapes, in_specs=[any_spec] * 5, out_spe...  116 us
    pallas_call x1, Pallas kernels, body(): pl.pallas_call(store, out_shape=shapes, in_specs=[any_spec] * 5, out_spec...  2.98 us

profile of v4, /device:TPU:0, one launch (start us, length us, event | category | flops | bytes accessed | tf_op | source)
XLA Modules:
  0.0 119.5 jit_solution(2399439113925621421)
XLA Ops:
  0.6 115.7 %shard_map.92 = (bf16[16,4096]{1,0:T(8,128)(2,1)}, bf16[16,4096]{1,0:T(8,128)(2,1)}, bf16[448,1024]{1,0:T(8,128)(2,1)}, bf16[448,1024]{1,0:T(8,128)(2,1)}, bf16[448,1024]{1,0:T(8,128)(2,1)}) custom-call(bf16[16,4096]{1,0:T(8,128)(2,1)} %tok.1, bf16[16,4096]{1,0:T(8,128)(2,1)} %cot.1, bf16[448,4096]{1,0:T(8,128)(2,1)} %bitcast.4, bf16[448,4096]{1,0:T(8,128)(2,1)} %bitcast.5, ...), custom_call_target="tpu_custom_call" | custom-call | flops 16999999488 | bytes 15000000 | tf_op jit(solution)/shard_map/pallas_call | solution.py:534
  116.3 3.0 %shard_map.93 = (bf16[16,4096]{1,0:T(8,128)(2,1)}, bf16[16,4096]{1,0:T(8,128)(2,1)}, bf16[448,1024]{1,0:T(8,128)(2,1)}, bf16[448,1024]{1,0:T(8,128)(2,1)}, bf16[448,1024]{1,0:T(8,128)(2,1)}) custom-call(bf16[16,4096]{1,0:T(8,128)(2,1)} %get-tuple-element.15.refs_0_, bf16[16,4096]{1,0:T(8,128)(2,1)} %get-tuple-element.16.refs_1_, ...), custom_call_target="tpu_custom_call" | custom-call | tf_op jit(solution)/shard_map/pallas_call | solution.py:561

commit v5 on v4

--- a/solution.py
+++ b/solution.py
@@ -51,7 +51,7 @@
     def peer(h, da=0, db=0):
         return dev(*at(h, ring(me_a[h], da), ring(me_b[h], db)))
 
-    started = []
+    started, gathers = [], []
 
     def send(src, dst, s, r, to):
         cp = pltpu.make_async_remote_copy(
@@ -98,7 +98,8 @@
         return X.at[(base[u] + h,) + at(h, a, b) + (pl.ds(row, 16), cols[u])]
 
     def gsend(u, i, ref, to):
-        send(ref, ref, gs.at[u, i], gr.at[u, i], to)
+        gathers.append(send(ref, ref, gs.at[u, i], gr.at[u, i], to))
+        started.pop()
 
     LATE = (0,)
     RELAY = (1,)
@@ -494,6 +495,8 @@
     s_second(2)
     w_part(5, 0)
     w_part(5, 1)
+    for cp in gathers:
+        cp.wait_send()
     w_finish(0, 0)
     w_finish(0, 1)
     s_third(2)

time: 120 us -> 120 us (level)
  no operation moved by 1% of the time
where the time goes in v5:
time: 120 us; the launch traced here: 119 us
  Pallas kernels  119 us (99%)
    pallas_call x1, Pallas kernels, body(): pl.pallas_call(kernel, out_shape=shapes, in_specs=[any_spec] * 5, out_spe...  116 us
    pallas_call x1, Pallas kernels, body(): pl.pallas_call(store, out_shape=shapes, in_specs=[any_spec] * 5, out_spec...  2.98 us

profile of v5, /device:TPU:0, one launch (start us, length us, event | category | flops | bytes accessed | tf_op | source)
XLA Modules:
  0.0 119.5 jit_solution(15004508381504428062)
XLA Ops:
  0.6 115.7 %shard_map.92 = (bf16[16,4096]{1,0:T(8,128)(2,1)}, bf16[16,4096]{1,0:T(8,128)(2,1)}, bf16[448,1024]{1,0:T(8,128)(2,1)}, bf16[448,1024]{1,0:T(8,128)(2,1)}, bf16[448,1024]{1,0:T(8,128)(2,1)}) custom-call(bf16[16,4096]{1,0:T(8,128)(2,1)} %tok.1, bf16[16,4096]{1,0:T(8,128)(2,1)} %cot.1, bf16[448,4096]{1,0:T(8,128)(2,1)} %bitcast.4, bf16[448,4096]{1,0:T(8,128)(2,1)} %bitcast.5, ...), custom_call_target="tpu_custom_call" | custom-call | flops 16999999488 | bytes 15000000 | tf_op jit(solution)/shard_map/pallas_call | solution.py:537
  116.3 3.0 %shard_map.93 = (bf16[16,4096]{1,0:T(8,128)(2,1)}, bf16[16,4096]{1,0:T(8,128)(2,1)}, bf16[448,1024]{1,0:T(8,128)(2,1)}, bf16[448,1024]{1,0:T(8,128)(2,1)}, bf16[448,1024]{1,0:T(8,128)(2,1)}) custom-call(bf16[16,4096]{1,0:T(8,128)(2,1)} %get-tuple-element.15.refs_0_, bf16[16,4096]{1,0:T(8,128)(2,1)} %get-tuple-element.16.refs_1_, ...), custom_call_target="tpu_custom_call" | custom-call | tf_op jit(solution)/shard_map/pallas_call | solution.py:564
